TPU v7x, 32 devices: a whole 2x2x4 slice. The times are simulated.
32 devices in a mesh: groups: 2 (over x), tensor: 16 (over z, y, core).
Axes of the slice: x: 2, y: 2, z: 4, core: 2. Of those that a mesh axis runs over, the one named last changes fastest.
Arguments:
- tile_cols: int32 [16, 2], P('groups'), parts along dimension 0, may hold values from 0 to 7, as said below
- pair_list: int32 [8], P('groups'), parts along dimension 0, may hold values from 0 to 3, each once
- amplitudes: bfloat16 [8, 8, 2, 9216], P('groups', None, None, 'tensor'), parts along dimension 0, may hold values from -6 to 6
- factors: bfloat16 [2304, 16, 2, 9216], P('tensor', 'groups'), parts along dimension 1, may hold values from -0.09375 to 0.09375
Outputs:
- residual: float32 [8, 8, 2, 9216], P('groups', None, None, 'tensor'), parts along dimension 0
There are 2 independent parts, one for each index of `groups`. A program takes and returns all parts, laid end to end along the dimension named above; each array names one. Nothing has to cross between parts.
Inputs may be any that keep to these rules, and one draw needn't show every extreme that they name: `tile_cols`: each row names 2 different tiles, the first being the row's own tile. `pair_list`: each stored pair once.
All inputs are finite; a program needn't handle non-finite values.
Results may differ from a plain program's by a relative error of at most 0.0028.
Values may be sent and summed in bfloat16 or wider, within the bound.
A program may use at most 256 MiB of HBM per device.

v0:
```python
import jax
import jax.numpy as jnp
from jax import lax
from jax.sharding import PartitionSpec as P

W = 96
NT = 8
KB = 2


def collect(chosen):
    return lax.all_gather(chosen, "tensor", axis=3, tiled=True)


def settle(partial_value):
    summed = lax.psum(partial_value, "tensor")
    share_len = partial_value.shape[3] // lax.axis_size("tensor")
    return lax.dynamic_slice_in_dim(summed, lax.axis_index("tensor") * share_len, share_len, 3)


def on_device(tile_cols, pair_list, amplitudes, factors):
    reached = tile_cols[tile_cols]
    matches = (reached[:, :, None, None, :] == reached[:, None, :, :, None]).astype(jnp.bfloat16)
    selector = (tile_cols[:, :, None] == jnp.arange(NT, dtype=jnp.int32)[None, None, :]).astype(
        jnp.bfloat16
    )
    aux_local = factors.shape[0]
    block_size = 1
    for candidate in range(1, 9):
        if aux_local % candidate == 0:
            block_size = candidate
    block_count = aux_local // block_size
    blocked = factors.reshape(block_count, block_size, NT, KB, W * W)
    chosen = jnp.take(amplitudes, pair_list, axis=0)
    routed = collect(chosen).reshape(-1, NT, KB, W, W)[:, tile_cols]
    picked = jnp.einsum(
        "aikjm,saimvw->saikjvw", matches, routed, preferred_element_type=jnp.float32
    )
    partial_picked = picked.astype(jnp.bfloat16)
    slot_count = partial_picked.shape[0]

    def advance(total, aux_block):
        factor_tiles = aux_block.reshape(block_size, NT, KB, W, W)
        half_done = jnp.einsum(
            "paiuv,saikjvw->spakjuw",
            factor_tiles,
            partial_picked,
            preferred_element_type=jnp.float32,
        )
        half_done = half_done.astype(jnp.bfloat16)
        partner = jnp.einsum(
            "akc,pcjxw->pakjxw", selector, factor_tiles, preferred_element_type=jnp.float32
        )
        partner = partner.astype(jnp.bfloat16)
        update = jnp.einsum(
            "spakjuw,pakjxw->sakux", half_done, partner, preferred_element_type=jnp.float32
        )
        return (total + update, None)

    start = jnp.zeros((slot_count, NT, KB, W, W), jnp.float32)
    total, unused = lax.scan(advance, start, blocked)
    return settle(total.reshape(slot_count, NT, KB, W * W))


def solution(mesh):
    placed = (
        P("groups", None),
        P("groups"),
        P("groups", None, None, "tensor"),
        P("tensor", "groups", None, None),
    )
    return jax.shard_map(
        on_device,
        mesh=mesh,
        in_specs=placed,
        out_specs=P("groups", None, None, "tensor"),
        check_vma=False,
    )
```

profile of v0, /device:TPU:0, one launch (start us, length us, event | category | flops | bytes accessed | tf_op | source)
XLA Modules:
  0.0 847.6 jit_solution(10867895129757116985)
XLA Ops:
  12.6 29.9 %copy.36 = bf16[144,8,2,9216]{3,1,2,0:T(8,128)(2,1)} copy(bf16[144,8,2,9216]{3,2,1,0:T(2,128)(2,1)} %param.9) | data formatting | bytes 84934656 | tf_op args[3]
  43.0 69.7 %all-gather.2.cloned.1.call-done = bf16[4,8,2,9216]{1,0,2,3:T(4,128)(2,1)} async-done(((bf16[4,8,2,576]{1,0,2,3:T(4,128)(2,1)}), bf16[4,8,2,9216]{1,0,2,3:T(4,128)(2,1)}) %all-gather.2.cloned.1.call-update) | async-done | bytes 1179664 | tf_op jit(solution)/shard_map/all_gather | solution.py:12
  112.7 21.2 %copy.56 = bf16[4,8,2,96,96]{4,3,2,0,1:T(8,128)(2,1)S(1)} copy(bf16[4,8,2,96,96]{1,0,2,4,3:T(4,128)(2,1)} %bitcast.84) | data formatting | bytes 2359296 | tf_op jit(solution)/shard_map/reshape | solution.py:35
  136.5 10.3 %fusion.25 = bf16[4,8,2,2,2,96,96]{6,4,3,5,0,2,1:T(2,128)(2,1)S(1)} fusion(bf16[8,2,4,2,96,96]{5,4,3,2,1,0:T(8,128)(2,1)} %bitcast.85, s32[8,2,2]{2,1,0:T(2,128)S(1)} %bitcast.86), kind=kOutput, calls=%fused_computation.20 | convolution fusion | flops 11796608 | bytes 7078016 | tf_op jit(solution)/shard_map/aikjm,saimvw->saikjvw/dot_general | solution.py:36
  151.3 581.9 %while.11 = (s32[]{:T(128)}, f32[4,8,2,96,96]{3,4,0,2,1:T(8,128)}, bf16[18,8,8,2,9216]{4,2,3,1,0:T(8,128)(2,1)}, bf16[4,8,2,2,2,96,96]{6,5,2,4,0,3,1:T(8,128)(2,...) while((s32[]{:T(128)}, f32[4,8,2,96,96]{3,4,0,2,1:T(8,128)}, ...), condition=%wide.region_1.2_spmd.clone, body=%wide.region_0.1_spmd.clone.sunk | while | flops 5486542848 | bytes 33030308 | solution.py:61
  163.5 19.9 %bitcast_add_fusion.2 = f32[4,8,2,96,96]{3,4,0,2,1:T(8,128)} fusion(f32[4,8,2,96,96]{3,4,0,2,1:T(8,128)} %get-tuple-element.123, bf16[4,8,2,2,2,96,96]{6,5,2,4,0,3,1:T(8,128)(2,1)} %get-tuple-element.132, bf16[8,8,2,2,96,96,1]{5,1,2,4,3,0,6:T(8,128)(2,1)} %convert_bitcast_fusion.2, pred[]{:T(512)S(6)} %compare.3, ...), kind=kOutput, calls=%fused_computation.11.clone.1 | convolution fusion | flops 5446434816 | bytes 16515073 | tf_op jit(solution)/shard_map/while/body/eval_jaxpr/spakjuw,pakjxw->sakux/dot_general | solution.py:55
  195.6 20.1 %bitcast_add_fusion.2 = f32[4,8,2,96,96]{3,4,0,2,1:T(8,128)} fusion(f32[4,8,2,96,96]{3,4,0,2,1:T(8,128)} %get-tuple-element.123, bf16[4,8,2,2,2,96,96]{6,5,2,4,0,3,1:T(8,128)(2,1)} %get-tuple-element.132, bf16[8,8,2,2,96,96,1]{5,1,2,4,3,0,6:T(8,128)(2,1)} %convert_bitcast_fusion.2, pred[]{:T(512)S(6)} %compare.3, ...), kind=kOutput, calls=%fused_computation.11.clone.1 | convolution fusion | flops 5446434816 | bytes 16515073 | tf_op jit(solution)/shard_map/while/body/eval_jaxpr/spakjuw,pakjxw->sakux/dot_general | solution.py:55
  228.0 20.1 %bitcast_add_fusion.2 = f32[4,8,2,96,96]{3,4,0,2,1:T(8,128)} fusion(f32[4,8,2,96,96]{3,4,0,2,1:T(8,128)} %get-tuple-element.123, bf16[4,8,2,2,2,96,96]{6,5,2,4,0,3,1:T(8,128)(2,1)} %get-tuple-element.132, bf16[8,8,2,2,96,96,1]{5,1,2,4,3,0,6:T(8,128)(2,1)} %convert_bitcast_fusion.2, pred[]{:T(512)S(6)} %compare.3, ...), kind=kOutput, calls=%fused_computation.11.clone.1 | convolution fusion | flops 5446434816 | bytes 16515073 | tf_op jit(solution)/shard_map/while/body/eval_jaxpr/spakjuw,pakjxw->sakux/dot_general | solution.py:55
  260.3 20.1 %bitcast_add_fusion.2 = f32[4,8,2,96,96]{3,4,0,2,1:T(8,128)} fusion(f32[4,8,2,96,96]{3,4,0,2,1:T(8,128)} %get-tuple-element.123, bf16[4,8,2,2,2,96,96]{6,5,2,4,0,3,1:T(8,128)(2,1)} %get-tuple-element.132, bf16[8,8,2,2,96,96,1]{5,1,2,4,3,0,6:T(8,128)(2,1)} %convert_bitcast_fusion.2, pred[]{:T(512)S(6)} %compare.3, ...), kind=kOutput, calls=%fused_computation.11.clone.1 | convolution fusion | flops 5446434816 | bytes 16515073 | tf_op jit(solution)/shard_map/while/body/eval_jaxpr/spakjuw,pakjxw->sakux/dot_general | solution.py:55
  292.6 20.1 %bitcast_add_fusion.2 = f32[4,8,2,96,96]{3,4,0,2,1:T(8,128)} fusion(f32[4,8,2,96,96]{3,4,0,2,1:T(8,128)} %get-tuple-element.123, bf16[4,8,2,2,2,96,96]{6,5,2,4,0,3,1:T(8,128)(2,1)} %get-tuple-element.132, bf16[8,8,2,2,96,96,1]{5,1,2,4,3,0,6:T(8,128)(2,1)} %convert_bitcast_fusion.2, pred[]{:T(512)S(6)} %compare.3, ...), kind=kOutput, calls=%fused_computation.11.clone.1 | convolution fusion | flops 5446434816 | bytes 16515073 | tf_op jit(solution)/shard_map/while/body/eval_jaxpr/spakjuw,pakjxw->sakux/dot_general | solution.py:55
  325.0 20.1 %bitcast_add_fusion.2 = f32[4,8,2,96,96]{3,4,0,2,1:T(8,128)} fusion(f32[4,8,2,96,96]{3,4,0,2,1:T(8,128)} %get-tuple-element.123, bf16[4,8,2,2,2,96,96]{6,5,2,4,0,3,1:T(8,128)(2,1)} %get-tuple-element.132, bf16[8,8,2,2,96,96,1]{5,1,2,4,3,0,6:T(8,128)(2,1)} %convert_bitcast_fusion.2, pred[]{:T(512)S(6)} %compare.3, ...), kind=kOutput, calls=%fused_computation.11.clone.1 | convolution fusion | flops 5446434816 | bytes 16515073 | tf_op jit(solution)/shard_map/while/body/eval_jaxpr/spakjuw,pakjxw->sakux/dot_general | solution.py:55
  357.3 20.1 %bitcast_add_fusion.2 = f32[4,8,2,96,96]{3,4,0,2,1:T(8,128)} fusion(f32[4,8,2,96,96]{3,4,0,2,1:T(8,128)} %get-tuple-element.123, bf16[4,8,2,2,2,96,96]{6,5,2,4,0,3,1:T(8,128)(2,1)} %get-tuple-element.132, bf16[8,8,2,2,96,96,1]{5,1,2,4,3,0,6:T(8,128)(2,1)} %convert_bitcast_fusion.2, pred[]{:T(512)S(6)} %compare.3, ...), kind=kOutput, calls=%fused_computation.11.clone.1 | convolution fusion | flops 5446434816 | bytes 16515073 | tf_op jit(solution)/shard_map/while/body/eval_jaxpr/spakjuw,pakjxw->sakux/dot_general | solution.py:55
  389.7 20.1 %bitcast_add_fusion.2 = f32[4,8,2,96,96]{3,4,0,2,1:T(8,128)} fusion(f32[4,8,2,96,96]{3,4,0,2,1:T(8,128)} %get-tuple-element.123, bf16[4,8,2,2,2,96,96]{6,5,2,4,0,3,1:T(8,128)(2,1)} %get-tuple-element.132, bf16[8,8,2,2,96,96,1]{5,1,2,4,3,0,6:T(8,128)(2,1)} %convert_bitcast_fusion.2, pred[]{:T(512)S(6)} %compare.3, ...), kind=kOutput, calls=%fused_computation.11.clone.1 | convolution fusion | flops 5446434816 | bytes 16515073 | tf_op jit(solution)/shard_map/while/body/eval_jaxpr/spakjuw,pakjxw->sakux/dot_general | solution.py:55
  422.0 20.1 %bitcast_add_fusion.2 = f32[4,8,2,96,96]{3,4,0,2,1:T(8,128)} fusion(f32[4,8,2,96,96]{3,4,0,2,1:T(8,128)} %get-tuple-element.123, bf16[4,8,2,2,2,96,96]{6,5,2,4,0,3,1:T(8,128)(2,1)} %get-tuple-element.132, bf16[8,8,2,2,96,96,1]{5,1,2,4,3,0,6:T(8,128)(2,1)} %convert_bitcast_fusion.2, pred[]{:T(512)S(6)} %compare.3, ...), kind=kOutput, calls=%fused_computation.11.clone.1 | convolution fusion | flops 5446434816 | bytes 16515073 | tf_op jit(solution)/shard_map/while/body/eval_jaxpr/spakjuw,pakjxw->sakux/dot_general | solution.py:55
  454.3 20.1 %bitcast_add_fusion.2 = f32[4,8,2,96,96]{3,4,0,2,1:T(8,128)} fusion(f32[4,8,2,96,96]{3,4,0,2,1:T(8,128)} %get-tuple-element.123, bf16[4,8,2,2,2,96,96]{6,5,2,4,0,3,1:T(8,128)(2,1)} %get-tuple-element.132, bf16[8,8,2,2,96,96,1]{5,1,2,4,3,0,6:T(8,128)(2,1)} %convert_bitcast_fusion.2, pred[]{:T(512)S(6)} %compare.3, ...), kind=kOutput, calls=%fused_computation.11.clone.1 | convolution fusion | flops 5446434816 | bytes 16515073 | tf_op jit(solution)/shard_map/while/body/eval_jaxpr/spakjuw,pakjxw->sakux/dot_general | solution.py:55
  486.7 20.1 %bitcast_add_fusion.2 = f32[4,8,2,96,96]{3,4,0,2,1:T(8,128)} fusion(f32[4,8,2,96,96]{3,4,0,2,1:T(8,128)} %get-tuple-element.123, bf16[4,8,2,2,2,96,96]{6,5,2,4,0,3,1:T(8,128)(2,1)} %get-tuple-element.132, bf16[8,8,2,2,96,96,1]{5,1,2,4,3,0,6:T(8,128)(2,1)} %convert_bitcast_fusion.2, pred[]{:T(512)S(6)} %compare.3, ...), kind=kOutput, calls=%fused_computation.11.clone.1 | convolution fusion | flops 5446434816 | bytes 16515073 | tf_op jit(solution)/shard_map/while/body/eval_jaxpr/spakjuw,pakjxw->sakux/dot_general | solution.py:55
  519.0 20.1 %bitcast_add_fusion.2 = f32[4,8,2,96,96]{3,4,0,2,1:T(8,128)} fusion(f32[4,8,2,96,96]{3,4,0,2,1:T(8,128)} %get-tuple-element.123, bf16[4,8,2,2,2,96,96]{6,5,2,4,0,3,1:T(8,128)(2,1)} %get-tuple-element.132, bf16[8,8,2,2,96,96,1]{5,1,2,4,3,0,6:T(8,128)(2,1)} %convert_bitcast_fusion.2, pred[]{:T(512)S(6)} %compare.3, ...), kind=kOutput, calls=%fused_computation.11.clone.1 | convolution fusion | flops 5446434816 | bytes 16515073 | tf_op jit(solution)/shard_map/while/body/eval_jaxpr/spakjuw,pakjxw->sakux/dot_general | solution.py:55
  551.3 20.1 %bitcast_add_fusion.2 = f32[4,8,2,96,96]{3,4,0,2,1:T(8,128)} fusion(f32[4,8,2,96,96]{3,4,0,2,1:T(8,128)} %get-tuple-element.123, bf16[4,8,2,2,2,96,96]{6,5,2,4,0,3,1:T(8,128)(2,1)} %get-tuple-element.132, bf16[8,8,2,2,96,96,1]{5,1,2,4,3,0,6:T(8,128)(2,1)} %convert_bitcast_fusion.2, pred[]{:T(512)S(6)} %compare.3, ...), kind=kOutput, calls=%fused_computation.11.clone.1 | convolution fusion | flops 5446434816 | bytes 16515073 | tf_op jit(solution)/shard_map/while/body/eval_jaxpr/spakjuw,pakjxw->sakux/dot_general | solution.py:55
  583.7 20.1 %bitcast_add_fusion.2 = f32[4,8,2,96,96]{3,4,0,2,1:T(8,128)} fusion(f32[4,8,2,96,96]{3,4,0,2,1:T(8,128)} %get-tuple-element.123, bf16[4,8,2,2,2,96,96]{6,5,2,4,0,3,1:T(8,128)(2,1)} %get-tuple-element.132, bf16[8,8,2,2,96,96,1]{5,1,2,4,3,0,6:T(8,128)(2,1)} %convert_bitcast_fusion.2, pred[]{:T(512)S(6)} %compare.3, ...), kind=kOutput, calls=%fused_computation.11.clone.1 | convolution fusion | flops 5446434816 | bytes 16515073 | tf_op jit(solution)/shard_map/while/body/eval_jaxpr/spakjuw,pakjxw->sakux/dot_general | solution.py:55
  616.0 20.1 %bitcast_add_fusion.2 = f32[4,8,2,96,96]{3,4,0,2,1:T(8,128)} fusion(f32[4,8,2,96,96]{3,4,0,2,1:T(8,128)} %get-tuple-element.123, bf16[4,8,2,2,2,96,96]{6,5,2,4,0,3,1:T(8,128)(2,1)} %get-tuple-element.132, bf16[8,8,2,2,96,96,1]{5,1,2,4,3,0,6:T(8,128)(2,1)} %convert_bitcast_fusion.2, pred[]{:T(512)S(6)} %compare.3, ...), kind=kOutput, calls=%fused_computation.11.clone.1 | convolution fusion | flops 5446434816 | bytes 16515073 | tf_op jit(solution)/shard_map/while/body/eval_jaxpr/spakjuw,pakjxw->sakux/dot_general | solution.py:55
  648.4 20.1 %bitcast_add_fusion.2 = f32[4,8,2,96,96]{3,4,0,2,1:T(8,128)} fusion(f32[4,8,2,96,96]{3,4,0,2,1:T(8,128)} %get-tuple-element.123, bf16[4,8,2,2,2,96,96]{6,5,2,4,0,3,1:T(8,128)(2,1)} %get-tuple-element.132, bf16[8,8,2,2,96,96,1]{5,1,2,4,3,0,6:T(8,128)(2,1)} %convert_bitcast_fusion.2, pred[]{:T(512)S(6)} %compare.3, ...), kind=kOutput, calls=%fused_computation.11.clone.1 | convolution fusion | flops 5446434816 | bytes 16515073 | tf_op jit(solution)/shard_map/while/body/eval_jaxpr/spakjuw,pakjxw->sakux/dot_general | solution.py:55
  680.7 20.1 %bitcast_add_fusion.2 = f32[4,8,2,96,96]{3,4,0,2,1:T(8,128)} fusion(f32[4,8,2,96,96]{3,4,0,2,1:T(8,128)} %get-tuple-element.123, bf16[4,8,2,2,2,96,96]{6,5,2,4,0,3,1:T(8,128)(2,1)} %get-tuple-element.132, bf16[8,8,2,2,96,96,1]{5,1,2,4,3,0,6:T(8,128)(2,1)} %convert_bitcast_fusion.2, pred[]{:T(512)S(6)} %compare.3, ...), kind=kOutput, calls=%fused_computation.11.clone.1 | convolution fusion | flops 5446434816 | bytes 16515073 | tf_op jit(solution)/shard_map/while/body/eval_jaxpr/spakjuw,pakjxw->sakux/dot_general | solution.py:55
  713.0 20.1 %bitcast_add_fusion.2 = f32[4,8,2,96,96]{3,4,0,2,1:T(8,128)} fusion(f32[4,8,2,96,96]{3,4,0,2,1:T(8,128)} %get-tuple-element.123, bf16[4,8,2,2,2,96,96]{6,5,2,4,0,3,1:T(8,128)(2,1)} %get-tuple-element.132, bf16[8,8,2,2,96,96,1]{5,1,2,4,3,0,6:T(8,128)(2,1)} %convert_bitcast_fusion.2, pred[]{:T(512)S(6)} %compare.3, ...), kind=kOutput, calls=%fused_computation.11.clone.1 | convolution fusion | flops 5446434816 | bytes 16515073 | tf_op jit(solution)/shard_map/while/body/eval_jaxpr/spakjuw,pakjxw->sakux/dot_general | solution.py:55
  739.6 99.3 %all-reduce.2.cloned.1.call-done = f32[4,8,2,9216]{3,2,1,0:T(2,128)} async-done(((f32[4,8,2,9216]{3,2,1,0:T(2,128)}), f32[4,8,2,9216]{3,2,1,0:T(2,128)}) %all-reduce.2.cloned.1.call-update) | async-done | bytes 2359312 | tf_op jit(solution)/shard_map/psum | solution.py:16
  (82 shorter events, 241.5 us)
Async XLA Ops:
  6.5 1.4 copy-start
  6.5 106.2 %all-gather.2.cloned.1.call-start = ((), (), s32[]{:S(2)}) async-start(), calls=%async_computation | async-start | bytes 20054016 | tf_op jit(solution)/shard_map/all_gather | solution.py:12
  10.9 828.0 %all-reduce.2.cloned.1.call-start = ((), (), s32[]{:S(2)}) async-start(), calls=%async_computation.1 | async-start | bytes 4718592 | tf_op jit(solution)/shard_map/psum | solution.py:16
  146.8 4.5 copy-start.2
  733.2 107.6 %copy-start.1 = (bf16[4,8,2,576]{3,2,1,0:T(2,128)(2,1)S(1)}, bf16[4,8,2,576]{3,2,1,0:T(2,128)(2,1)}, u32[]{:S(2)}) copy-start(bf16[4,8,2,576]{3,2,1,0:T(2,128)(2,1)} %param.8) | copy-start | bytes 221188
Sparse Core Ops, SparseCore 0:
  11.0 101.6 all-gather.1
  739.7 99.1 all-reduce.1
where the time goes:
time: 850 us; the launch traced here: 848 us
  matrix products  453 us (53%)
  local copies, waits for them, and re-layouts  209 us (25%)
  waiting for transfers between devices  169 us (20%)
  between operations  13.5 us (2%)
    dot_general x18, matrix products, advance(): jnp.einsum('spakjuw,pakjxw->sakux', half_done, partner, preferred_element...  362 us
    psum x1, waiting for transfers between devices, settle(): summed = lax.psum(partial_value, 'tensor')  99.3 us
    dot_general x18, matrix products, advance(): jnp.einsum('akc,pcjxw->pakjxw', selector, factor_tiles, preferred_element...  81.1 us
    reshape x18, local copies, waits for them, and re-layouts, advance(): factor_tiles = aux_block.reshape(block_size, NT, KB, W, W)  80.4 us
    all_gather x1, waiting for transfers between devices, collect(): return lax.all_gather(chosen, 'tensor', axis=3, tiled=True)  69.7 us
    dynamic_slice x18, local copies, waits for them, and re-layouts, on_device(): total, unused = lax.scan(advance, start, blocked)  58.2 us
    unnamed x9, local copies, waits for them, and re-layouts  35.1 us
    reshape x1, local copies, waits for them, and re-layouts, on_device(): routed = collect(chosen).reshape(-1, NT, KB, W, W)[:, tile_cols]  21.2 us
  transfers between devices with their start and end apart: 2, of which 2 were waited for; matrix products, arithmetic and copies ran while one was open for 4% of the time, Pallas kernels for 0%

commit v1 on v0

v1 whole, which is shorter than its diff:
```python
import functools

import jax
import jax.numpy as jnp
from jax import lax
from jax.experimental import pallas as pl
from jax.experimental.pallas import tpu as pltpu
from jax.sharding import PartitionSpec as P

W = 96
NT = 8
KB = 2
LANES = 128
WIDE = KB * LANES
CHUNKS = W * W // LANES
GROUP = W // 4
HALVES = 2
VMEM = 56 * 1024 * 1024


def lay_kernel(block, x_ref, y_ref, flat_ref, tile_ref):
    lane = lax.broadcasted_iota(jnp.int32, (GROUP, LANES), 1)

    def one(p, carry):
        for a in range(NT):
            flat_ref[a] = x_ref[p, a].astype(jnp.float32)
            for k in range(KB):
                first, second, third = (
                    flat_ref[a, pl.ds(KB * j + k, GROUP, stride=3 * KB), :] for j in range(3)
                )
                rows = (
                    first,
                    pltpu.roll(jnp.where(lane >= 96, first, second), 32, 1),
                    pltpu.roll(jnp.where(lane >= 64, second, third), 64, 1),
                    pltpu.roll(third, 96, 1),
                )
                for r in range(4):
                    tile_ref[a, k, pl.ds(r, GROUP, stride=4), :] = jnp.where(lane < W, rows[r], 0.0)
            for k in range(KB):
                y_ref[p, a, :, k * LANES : (k + 1) * LANES] = tile_ref[a, k].astype(jnp.bfloat16)
        return carry

    lax.fori_loop(0, block, one, 0)


def lay(flat):
    count = flat.shape[0]
    block = max(c for c in (1, 2, 3, 4, 6, 8) if count % c == 0)
    chunked = flat.reshape(count, NT, KB, CHUNKS, LANES).transpose(0, 1, 3, 2, 4)
    chunked = chunked.reshape(count, NT, CHUNKS * KB, LANES)
    return pl.pallas_call(
        functools.partial(lay_kernel, block),
        grid=(count // block,),
        in_specs=[pl.BlockSpec((block, NT, CHUNKS * KB, LANES), lambda i: (i, 0, 0, 0))],
        out_specs=pl.BlockSpec((block, NT, W, WIDE), lambda i: (i, 0, 0, 0)),
        scratch_shapes=[
            pltpu.VMEM((NT, CHUNKS * KB, LANES), jnp.float32),
            pltpu.VMEM((NT, KB, W, LANES), jnp.float32),
        ],
        out_shape=jax.ShapeDtypeStruct((count, NT, W, WIDE), jnp.bfloat16),
        compiler_params=pltpu.CompilerParams(vmem_limit_bytes=VMEM),
        cost_estimate=pl.CostEstimate(
            flops=flat.size, bytes_accessed=flat.size * 5, transcendentals=0
        ),
    )(chunked)


def ladder_kernel(slots, block, first, count, near_ref, b_ref, tile_ref, out_ref, half_ref, t_ref):
    stride = 3 * LANES

    @pl.when(pl.program_id(0) == 0)
    def _():
        out_ref[...] = jnp.zeros_like(out_ref)
        t_ref[...] = jnp.zeros_like(t_ref)
        for i in range(count):
            near = near_ref[first + i]
            closed = near_ref[near] == first + i
            for s in range(slots):
                at = s * stride
                own = tile_ref[s, first + i]
                beside = tile_ref[s, near]
                t_ref[i, 0:W, at : at + WIDE] = own
                t_ref[i, LANES : LANES + W, at + LANES : at + LANES + WIDE] = beside

                @pl.when(closed)
                def _():
                    t_ref[i, 0:W, at + WIDE : at + stride] = tile_ref[s, first + i, :, 0:LANES]
                    t_ref[i, LANES : LANES + W, at : at + LANES] = tile_ref[s, near, :, LANES:WIDE]

    def form(i):
        for p in range(block):
            half = lax.dot_general(
                b_ref[p, first + i],
                t_ref[i],
                (((1,), (0,)), ((), ())),
                preferred_element_type=jnp.float32,
            ).astype(jnp.bfloat16)
            for s in range(slots):
                half_ref[i % 2, p, s * W : (s + 1) * W, :] = half[:, s * stride : (s + 1) * stride]

    def close(i):
        near = near_ref[first + i]
        for k, d in ((0, first + i), (1, near)):
            left = jnp.concatenate(
                [half_ref[i % 2, p, :, k * LANES : k * LANES + WIDE] for p in range(block)], axis=1
            )
            right = jnp.concatenate([b_ref[p, d] for p in range(block)], axis=1)
            part = lax.dot_general(
                left, right, (((1,), (1,)), ((), ())), preferred_element_type=jnp.float32
            )
            for s in range(slots):
                out_ref[s, i, k] += part[s * W : (s + 1) * W]

    for i in range(count):
        form(i)
        if i:
            close(i - 1)
    close(count - 1)


def ladder(near, rows, tiles, first, count):
    aux, slots = rows.shape[0], tiles.shape[0]
    block = max(c for c in (1, 2, 3, 4, 6, 8) if aux % c == 0)
    return pl.pallas_call(
        functools.partial(ladder_kernel, slots, block, first, count),
        grid_spec=pltpu.PrefetchScalarGridSpec(
            num_scalar_prefetch=1,
            grid=(aux // block,),
            in_specs=[
                pl.BlockSpec((block, NT, W, WIDE), lambda i, near: (i, 0, 0, 0)),
                pl.BlockSpec(memory_space=pltpu.VMEM),
            ],
            out_specs=pl.BlockSpec((slots, count, KB, W, W), lambda i, near: (0, 0, 0, 0, 0)),
            scratch_shapes=[
                pltpu.VMEM((2, block, slots * W, 3 * LANES), jnp.bfloat16),
                pltpu.VMEM((count, WIDE, slots * 3 * LANES), jnp.bfloat16),
            ],
        ),
        out_shape=jax.ShapeDtypeStruct((slots, count, KB, W, W), jnp.float32),
        compiler_params=pltpu.CompilerParams(vmem_limit_bytes=VMEM),
        cost_estimate=pl.CostEstimate(
            flops=aux * count * slots * 8 * 2 * W**3, bytes_accessed=rows.size * 2, transcendentals=0
        ),
    )(near, rows, tiles)


def settle(part, merged):
    size = lax.axis_size("tensor")
    slots, count = part.shape[:2]
    tile = (W * W,) if W % size else (W, W)
    lead = ((slots, count, KB), (slots, count * KB), (slots * count * KB,))[merged]
    share = lax.psum_scatter(
        part.reshape(lead + tile), "tensor", scatter_dimension=len(lead), tiled=True
    )
    return share.reshape(slots, count, KB, W * W // size)


def on_device(tile_cols, pair_list, amplitudes, factors):
    chosen = jnp.take(amplitudes, pair_list, axis=0)
    slots, share = chosen.shape[0], chosen.shape[3]
    pieces = lax.all_gather(chosen.reshape(slots * NT * KB, share), "tensor")
    tiles = lay(pieces.transpose(1, 0, 2).reshape(slots, NT, KB, W * W))
    rows = lay(factors)
    near = tile_cols[:, 1]
    count = NT // HALVES
    shares = [settle(ladder(near, rows, tiles, h * count, count), h) for h in range(HALVES)]
    return jnp.concatenate(shares, axis=1)


def solution(mesh):
    placed = (
        P("groups", None),
        P("groups"),
        P("groups", None, None, "tensor"),
        P("tensor", "groups", None, None),
    )
    return jax.shard_map(
        on_device,
        mesh=mesh,
        in_specs=placed,
        out_specs=P("groups", None, None, "tensor"),
        check_vma=False,
    )
```

time: 850 us -> 419 us (0.49)
  matrix products: 453 us -> 0 us
  Pallas kernels: 0 us -> 324 us
  local copies, waits for them, and re-layouts: 209 us -> 17.5 us
  waiting for transfers between devices: 169 us -> 59.3 us
    dot_general x37 -> x0, matrix products: 453 us -> none  [the longest x18 362 us: advance(): jnp.einsum('spakjuw,pakjxw->sakux', half_done, partner, preferred_element...]
    pallas_call x0 -> x4, Pallas kernels: none -> 324 us  [the longest x2 275 us: ladder(): pl.pallas_call(functools.partial(ladder_kernel, slots, block, first, coun...]
    reshape x20 -> x3, local copies, waits for them, and re-layouts: 106 us -> 3.83 us  [the longest x1 3.56 us: settle(): part.reshape(lead + tile)]
    psum x1 -> x0, waiting for transfers between devices: 99.3 us -> none  [settle(): summed = lax.psum(partial_value, 'tensor')]
    all_gather x1, waiting for transfers between devices: 69.7 us -> 0.01 us  [on_device(): pieces = lax.all_gather(chosen.reshape(slots * NT * KB, share), 'tensor')]
    dynamic_slice x19 -> x0, local copies, waits for them, and re-layouts: 60 us -> none  [the longest x18 58.2 us: on_device(): total, unused = lax.scan(advance, start, blocked)]
    reduce_scatter x0 -> x1, waiting for transfers between devices: none -> 59.2 us  [settle(): lax.psum_scatter(part.reshape(lead + tile), 'tensor', scatter_dimension=l...]
    unnamed x9 -> x10, local copies, waits for them, and re-layouts: 35.1 us -> 2.13 us
  transfers between devices with their start and end apart: 2 -> 3, of which waited for: 2 -> 1; matrix products, arithmetic and copies ran while one was open for 4% -> 1% of each run, Pallas kernels for 0% -> 44%
where the time goes in v1:
time: 419 us; the launch traced here: 418 us
  Pallas kernels  324 us (77%)
  waiting for transfers between devices  59.3 us (14%)
  local copies, waits for them, and re-layouts  17.5 us (4%)
  between operations  13.8 us (3%)
    pallas_call x2, Pallas kernels, ladder(): pl.pallas_call(functools.partial(ladder_kernel, slots, block, first, coun...  275 us
    reduce_scatter x1, waiting for transfers between devices, settle(): lax.psum_scatter(part.reshape(lead + tile), 'tensor', scatter_dimension=l...  59.2 us
    pallas_call x2, Pallas kernels, lay(): pl.pallas_call(functools.partial(lay_kernel, block), grid=(count // block...  48.5 us
  transfers between devices with their start and end apart: 3, of which 1 were waited for; matrix products, arithmetic and copies ran while one was open for 1% of the time, Pallas kernels for 44%

profile of v1, /device:TPU:0, one launch (start us, length us, event | category | flops | bytes accessed | tf_op | source)
XLA Modules:
  0.0 417.6 jit_solution(4850124018221781529)
XLA Ops:
  6.5 0.7 compare_select_fusion
  7.2 0.7 compare_and_fusion
  7.9 0.7 gather_fusion
  8.8 0.1 broadcast_in_dim.17
  8.9 0.7 broadcast_select_fusion
  9.7 45.1 %shard_map.46.b_ref = bf16[144,8,96,256]{3,2,1,0:T(8,128)(2,1)} custom-call(bf16[144,8,144,128]{3,2,1,0:T(8,128)(2,1)} %bitcast.12), custom_call_target="tpu_custom_call" | custom-call | flops 21233664 | bytes 106168320 | tf_op jit(solution)/shard_map/pallas_call | solution.py:51
  54.8 0.6 slice_bitcast_fusion.near_ref
  55.4 2.1 copy.10
  57.5 1.4 reshape_reshape.3
  58.9 1.9 copy.11
  60.8 3.4 shard_map.47.tile_ref
  64.2 137.7 %shard_map.48 = f32[4,4,2,96,96]{4,3,2,1,0:T(8,128)} custom-call(s32[8]{0:T(128)} %slice_bitcast_fusion.near_ref, bf16[144,8,96,256]{3,2,1,0:T(8,128)(2,1)} %shard_map.46.b_ref, bf16[4,8,96,256]{3,2,1,0:T(8,128)(2,1)} %shard_map.47.tile_ref), custom_call_target="tpu_custom_call" | custom-call | flops 32614907904 | bytes 56623104 | tf_op jit(solution)/shard_map/pallas_call | solution.py:124
  201.9 3.6 copy.12
  205.5 0.2 reduce-scatter.2.cloned.1.call-start
  205.7 137.7 %shard_map.49 = f32[4,4,2,96,96]{4,3,2,1,0:T(8,128)} custom-call(s32[8]{0:T(128)} %slice_bitcast_fusion.near_ref, bf16[144,8,96,256]{3,2,1,0:T(8,128)(2,1)} %shard_map.46.b_ref, bf16[4,8,96,256]{3,2,1,0:T(8,128)(2,1)} %shard_map.47.tile_ref), custom_call_target="tpu_custom_call" | custom-call | flops 32614907904 | bytes 56623104 | tf_op jit(solution)/shard_map/pallas_call | solution.py:124
  343.4 3.6 copy.14
  347.0 0.6 copy-done.3
  347.6 0.6 dynamic-slice
  348.9 0.9 constant_dynamic-slice_fusion
  349.9 0.1 reshape.58
  350.0 59.2 %reduce-scatter.2.cloned.1.call-done = f32[4,8,6,96]{3,1,0,2:T(8,128)} async-done(((f32[4,8,96,96]{3,1,0,2:T(8,128)}), f32[4,8,6,96]{3,1,0,2:T(8,128)}) %reduce-scatter.2.cloned.1.call-update) | async-done | bytes 73744 | tf_op jit(solution)/shard_map/reduce_scatter | solution.py:152
  409.2 1.0 copy.15
  410.2 0.1 reshape.60
  410.3 0.7 pad_maximum_fusion
  (18 shorter events, 0.3 us)
Async XLA Ops:
  6.5 1.4 copy-start
  6.5 48.9 %all-gather.2.cloned.1.call-start = ((), (), s32[]{:S(2)}) async-start(), calls=%async_computation.1 | async-start | bytes 1392640 | tf_op jit(solution)/shard_map/all_gather | solution.py:161
  9.7 339.2 %all-reduce.3.cloned.1.call-start = ((), (), s32[]{:S(2)}) async-start(), calls=%async_computation.3 | async-start | bytes 3145728
  9.7 45.1 %copy-start.2 = (s32[8,2]{0,1:T(2,128)S(1)}, s32[8,2]{0,1:T(2,128)}, u32[]{:S(2)}) copy-start(s32[8,2]{0,1:T(2,128)} %param.4) | copy-start | bytes 196
  205.5 203.7 %reduce-scatter.2.cloned.1.call-start = ((), (), s32[]{:S(2)}) async-start(), calls=%async_computation.2 | async-start | bytes 1671168 | tf_op jit(solution)/shard_map/reduce_scatter | solution.py:152
  343.4 67.7 %copy-start.1 = (bf16[4,8,2,576]{3,2,1,0:T(2,128)(2,1)S(1)}, bf16[4,8,2,576]{3,2,1,0:T(2,128)(2,1)}, u32[]{:S(2)}) copy-start(bf16[4,8,2,576]{3,2,1,0:T(2,128)(2,1)} %param.6) | copy-start | bytes 221188
  347.0 0.7 copy-start.3
Sparse Core Ops, SparseCore 0:
  9.8 41.4 all-gather.1
  205.6 97.9 all-reduce.2
  347.1 62.0 reduce-scatter.1
